TPU v7x, 32 devices: a whole 2x2x4 slice. The times are simulated.
32 devices in a mesh: gx: 4 (over z), gy: 2 (over y), gz: 4 (over x, core).
Axes of the slice: x: 2, y: 2, z: 4, core: 2. Of those that a mesh axis runs over, the one named last changes fastest.
Arguments:
- composition: float32 [12, 8, 16, 512], P(None, 'gx', 'gy', 'gz'), may hold values from -3 to 3
- cotangent: float32 [12, 8, 16, 512], P(None, 'gx', 'gy', 'gz'), may hold values from -4 to 4
- weight_one: bfloat16 [64, 12], replicated, may hold values from -1.75 to 1.75
- bias_one: float32 [64], replicated, may hold values from -0.5 to 0.5
- weight_two: bfloat16 [64, 64], replicated, may hold values from -0.75 to 0.75
- bias_two: float32 [64], replicated, may hold values from -0.5 to 0.5
- weight_three: bfloat16 [144, 64], replicated, may hold values from -0.75 to 0.75
- bias_three: float32 [144], replicated, may hold values from -1 to 1
Outputs:
- grad_composition: float32 [12, 8, 16, 512], P(None, 'gx', 'gy', 'gz')
- grad_weight_one: float32 [64, 12], replicated
- grad_bias_one: float32 [64], replicated
- grad_weight_two: float32 [64, 64], replicated
- grad_bias_two: float32 [64], replicated
- grad_weight_three: float32 [144, 64], replicated
- grad_bias_three: float32 [144], replicated
All inputs are finite; a program needn't handle non-finite values.
Results may differ from a plain program's by a relative error of at most 0.0077.
Values sent between devices are 32-bit elements; how exact they have to be, the bound alone decides.
A program may use at most 128 MiB of HBM per device.

v0:
```python
import math

import jax
import jax.numpy as jnp
from jax import lax
from jax.sharding import PartitionSpec as P

step_size = 0.08
cubic_coef = 0.1
diag_scale = 0.5
off_scale = 0.04


def extended_2(value, sides, width):
    for axis, dim in sides:
        size, length = (lax.axis_size(axis), value.shape[dim])
        up = [(i, (i + 1) % size) for i in range(size)]
        down = [(j, i) for i, j in up]
        last = lax.slice_in_dim(value, length - width, length, axis=dim)
        leading = lax.slice_in_dim(value, 0, width, axis=dim)
        before = lax.ppermute(last, axis, up)
        after = lax.ppermute(leading, axis, down)
        value = jnp.concatenate([before, value, after], axis=dim)
    return value


def potential(values):
    return values + cubic_coef * values * values * values


def potential_slope(values):
    return 1.0 + 3.0 * cubic_coef * values * values


def mobility_tables(channels):
    position = jnp.arange(channels * channels, dtype=jnp.int32)
    on_diagonal = position // channels == position % channels
    identity = jnp.where(on_diagonal, 1.0, 0.0).astype(jnp.float32)
    scales = jnp.where(on_diagonal, diag_scale, off_scale).astype(jnp.float32)
    return (identity, scales)


def forward_net(flattened, weights):
    weight_one, bias_one, weight_two, bias_two, weight_three, bias_three = weights
    identity, scales = mobility_tables(flattened.shape[0])
    inputs = flattened.astype(jnp.bfloat16)
    hidden_one = jnp.tanh(
        jnp.dot(weight_one, inputs, preferred_element_type=jnp.float32) + bias_one[:, None]
    ).astype(jnp.bfloat16)
    hidden_two = jnp.tanh(
        jnp.dot(weight_two, hidden_one, preferred_element_type=jnp.float32) + bias_two[:, None]
    ).astype(jnp.bfloat16)
    active = jnp.tanh(
        jnp.dot(weight_three, hidden_two, preferred_element_type=jnp.float32) + bias_three[:, None]
    )
    mobility = identity[:, None] + scales[:, None] * active
    return (mobility, (inputs, hidden_one, hidden_two, active))


def backward_net(grad_mob, stored, weights):
    weight_one, bias_one, weight_two, bias_two, weight_three, bias_three = weights
    inputs, hidden_one, hidden_two, active = stored
    _, scales = mobility_tables(inputs.shape[0])
    pre_three = (grad_mob * scales[:, None] * (1.0 - active * active)).astype(jnp.bfloat16)
    upper_two = hidden_two.astype(jnp.float32)
    pre_two = (
        jnp.dot(weight_three.T, pre_three, preferred_element_type=jnp.float32)
        * (1.0 - upper_two * upper_two)
    ).astype(jnp.bfloat16)
    upper_one = hidden_one.astype(jnp.float32)
    pre_one = (
        jnp.dot(weight_two.T, pre_two, preferred_element_type=jnp.float32)
        * (1.0 - upper_one * upper_one)
    ).astype(jnp.bfloat16)
    net_grad = jnp.dot(weight_one.T, pre_one, preferred_element_type=jnp.float32)
    grads = (
        jnp.dot(pre_one, inputs.T, preferred_element_type=jnp.float32),
        jnp.sum(pre_one.astype(jnp.float32), axis=1),
        jnp.dot(pre_two, hidden_one.T, preferred_element_type=jnp.float32),
        jnp.sum(pre_two.astype(jnp.float32), axis=1),
        jnp.dot(pre_three, hidden_two.T, preferred_element_type=jnp.float32),
        jnp.sum(pre_three.astype(jnp.float32), axis=1),
    )
    return (net_grad, grads)


def apply_mobility(mobility, vector):
    channels = vector.shape[0]
    matrix = mobility.reshape((channels, channels) + vector.shape[1:])
    return jnp.sum(matrix * vector[None], axis=1)


def apply_transpose(mobility, vector):
    channels = vector.shape[0]
    matrix = mobility.reshape((channels, channels) + vector.shape[1:])
    return jnp.sum(matrix * vector[:, None], axis=0)


def outer_terms(adjoint, pot_jump):
    channels = adjoint.shape[0]
    return (adjoint[:, None] * pot_jump[None]).reshape((channels * channels,) + adjoint.shape[1:])


def leading(values, spatial):
    return lax.slice_in_dim(values, 0, values.shape[spatial] - 1, axis=spatial)


def trailing(values, spatial):
    return lax.slice_in_dim(values, 1, values.shape[spatial], axis=spatial)


def along_axes(extended):
    return [extended[:, :, 1:-1, 1:-1], extended[:, 1:-1, :, 1:-1], extended[:, 1:-1, 1:-1, :]]


def face_slabs(extended):
    return [
        extended[:, 0, 1:-1, 1:-1],
        extended[:, -1, 1:-1, 1:-1],
        extended[:, 1:-1, 0, 1:-1],
        extended[:, 1:-1, -1, 1:-1],
        extended[:, 1:-1, 1:-1, 0],
        extended[:, 1:-1, 1:-1, -1],
    ]


def joined(lower_slab, inner_mob, upper_slab, spatial):
    return jnp.concatenate(
        [jnp.expand_dims(lower_slab, spatial), inner_mob, jnp.expand_dims(upper_slab, spatial)],
        axis=spatial,
    )


def cell_network(values, weights):
    channels = values.shape[0]
    mobility, stored = forward_net(values.reshape(channels, -1), weights)
    return (mobility.reshape((channels * channels,) + values.shape[1:]), stored)


def rim_mobility(extended, inner_mob, weights):
    slab_list = face_slabs(extended)
    channels = extended.shape[0]
    flattened = jnp.concatenate(
        [face_slab.reshape(channels, -1) for face_slab in slab_list], axis=1
    )
    rim_mob, _ = forward_net(flattened, weights)
    pieces = []
    offset = 0
    for face_slab in slab_list:
        length = face_slab.shape[1] * face_slab.shape[2]
        pieces.append(
            rim_mob[:, offset : offset + length].reshape((rim_mob.shape[0],) + face_slab.shape[1:])
        )
        offset = offset + length
    return [
        joined(pieces[0], inner_mob, pieces[1], 1),
        joined(pieces[2], inner_mob, pieces[3], 2),
        joined(pieces[4], inner_mob, pieces[5], 3),
    ]


def forward_update(current, pot_axes, mob_axes):
    change = jnp.zeros_like(current)
    for spatial, potentials, mobility in zip((1, 2, 3), pot_axes, mob_axes):
        face_mob = 0.5 * (leading(mobility, spatial) + trailing(mobility, spatial))
        pot_jump = trailing(potentials, spatial) - leading(potentials, spatial)
        face_flux = apply_mobility(face_mob, pot_jump)
        change = change + (trailing(face_flux, spatial) - leading(face_flux, spatial))
    return current + step_size * change


def backward_update(current, incoming, pot_axes, adj_axes, mob_axes, stored, weights):
    grad_pot = jnp.zeros_like(current)
    grad_mob = jnp.zeros(mob_axes[0].shape[:1] + current.shape[1:], jnp.float32)
    for spatial, potentials, adjoints, mobility in zip((1, 2, 3), pot_axes, adj_axes, mob_axes):
        face_mob = 0.5 * (leading(mobility, spatial) + trailing(mobility, spatial))
        pot_jump = trailing(potentials, spatial) - leading(potentials, spatial)
        adjoint = step_size * (leading(adjoints, spatial) - trailing(adjoints, spatial))
        back_flow = apply_transpose(face_mob, adjoint)
        outer_prod = outer_terms(adjoint, pot_jump)
        grad_pot = grad_pot + (leading(back_flow, spatial) - trailing(back_flow, spatial))
        grad_mob = grad_mob + (leading(outer_prod, spatial) + trailing(outer_prod, spatial))
    grad_mob = 0.5 * grad_mob
    net_grad, grads = backward_net(grad_mob.reshape(grad_mob.shape[0], -1), stored, weights)
    outgoing = incoming + grad_pot * potential_slope(current) + net_grad.reshape(current.shape)
    return (outgoing, grads)


def shards(
    composition, cotangent, weight_one, bias_one, weight_two, bias_two, weight_three, bias_three
):
    weights = (weight_one, bias_one, weight_two, bias_two, weight_three, bias_three)
    channels = composition.shape[0]
    rim_state = extended_2(composition, (("gx", 1), ("gy", 2), ("gz", 3)), 1)
    inner_mob, inner_stored = cell_network(composition, weights)
    mob_axes = rim_mobility(rim_state, inner_mob, weights)
    pot_axes = along_axes(potential(rim_state))
    moved = forward_update(composition, pot_axes, mob_axes)
    paired = extended_2(
        jnp.concatenate([moved, cotangent], axis=0), (("gx", 1), ("gy", 2), ("gz", 3)), 1
    )
    rim_moved = paired[:channels]
    rim_cot = paired[channels:]
    moved_mob, moved_stored = cell_network(moved, weights)
    moved_axes = rim_mobility(rim_moved, moved_mob, weights)
    back_one, grads_late = backward_update(
        moved,
        cotangent,
        along_axes(potential(rim_moved)),
        along_axes(rim_cot),
        moved_axes,
        moved_stored,
        weights,
    )
    late_total = lax.psum(
        (grads_late[0], grads_late[1], grads_late[2], grads_late[3], grads_late[4], grads_late[5]),
        ("gx", "gy", "gz"),
    )
    rim_back = extended_2(back_one, (("gx", 1), ("gy", 2), ("gz", 3)), 1)
    back_zero, grads_early = backward_update(
        composition, back_one, pot_axes, along_axes(rim_back), mob_axes, inner_stored, weights
    )
    early_total = lax.psum(
        (
            grads_early[0],
            grads_early[1],
            grads_early[2],
            grads_early[3],
            grads_early[4],
            grads_early[5],
        ),
        ("gx", "gy", "gz"),
    )
    totals = tuple((late + early for late, early in zip(late_total, early_total)))
    cell_total = (
        composition.shape[1]
        * lax.axis_size("gx")
        * composition.shape[2]
        * lax.axis_size("gy")
        * composition.shape[3]
        * lax.axis_size("gz")
    )
    factor = 1.0 / (step_size * math.sqrt(cell_total))
    scaled = tuple((member * factor for member in totals))
    return (back_zero, scaled[0], scaled[1], scaled[2], scaled[3], scaled[4], scaled[5])


def solution(mesh):
    in_specs = (P(None, "gx", "gy", "gz"), P(None, "gx", "gy", "gz"), P(), P(), P(), P(), P(), P())
    out_specs = (P(None, "gx", "gy", "gz"), P(), P(), P(), P(), P(), P())
    return jax.shard_map(shards, mesh=mesh, in_specs=in_specs, out_specs=out_specs, check_vma=False)
```

profile of v0, /device:TPU:12, one launch (start us, length us, event | category | flops | bytes accessed | tf_op | source)
XLA Modules:
  0.0 186.1 jit_solution(6180898263046738725)
XLA Ops:
  2.0 1.6 collective-permute-start
  3.6 4.6 %collective-permute-done = f32[12,1,8,128]{3,2,1,0:T(8,128)S(1)} collective-permute-done((f32[12,1,8,128]{3,2,1,0:T(8,128)S(1)}, f32[12,1,8,128]{3,2,1,0:T(8,128)S(1)}, u32[]{:S(2)}, u32[]{:S(2)}) %collective-permute-start) | collective-permute-done | bytes 49184 | tf_op jit(solution)/shard_map/ppermute | solution.py:21
  8.2 1.0 convert_bitcast_fusion.1
  9.8 1.5 collective-permute-start.2
  13.0 1.0 fusion.31
  16.3 10.8 %collective-permute-done.4 = f32[12,4,10,1]{3,2,1,0:T(8,128)S(1)} collective-permute-done((f32[12,4,10,1]{3,2,1,0:T(8,128)S(1)}, f32[12,4,10,1]{3,2,1,0:T(8,128)S(1)}, u32[]{:S(2)}, u32[]{:S(2)}) %collective-permute-start.4) | collective-permute-done | bytes 1952 | tf_op jit(solution)/shard_map/ppermute | solution.py:21
  28.7 1.1 fusion.13
  29.7 1.5 fusion.3
  32.0 1.7 multiply_add_fusion.1
  36.3 1.2 slice_bitcast_fusion.3
  38.2 1.7 reshape.158
  40.0 1.3 copy.514
  41.3 1.2 copy.511
  42.5 1.8 multiply_reduce_fusion.2
  46.3 3.3 %collective-permute-start.7 = (f32[24,1,8,128]{3,2,1,0:T(8,128)S(1)}, f32[24,1,8,128]{3,2,1,0:T(8,128)S(1)}, u32[]{:S(2)}, u32[]{:S(2)}) collective-permute-start(f32[24,1,8,128]{3,2,1,0:T(8,128)S(1)} %get-tuple-element.76), channel_id=1, source_target_pairs={{8,0},{16,8},{24,16},{0,24},{9,1},{17,9},{25,17},{1,25},{10,2},{18... | collective-permute-start | bytes 294920 | tf_op jit(solution)/shard_map/ppermute | solution.py:22
  50.6 2.2 %collective-permute-done.7 = f32[24,1,8,128]{3,2,1,0:T(8,128)S(1)} collective-permute-done((f32[24,1,8,128]{3,2,1,0:T(8,128)S(1)}, f32[24,1,8,128]{3,2,1,0:T(8,128)S(1)}, u32[]{:S(2)}, u32[]{:S(2)}) %collective-permute-start.7) | collective-permute-done | bytes 98336 | tf_op jit(solution)/shard_map/ppermute | solution.py:22
  52.9 1.5 collective-permute-done.6
  55.0 1.5 collective-permute-start.8
  57.3 1.0 copy.471
  60.2 1.0 copy.462
  63.1 1.0 broadcast_multiply_fusion.17
  68.4 1.5 copy.479
  69.9 1.4 multiply_add_fusion
  75.2 1.4 copy.464
  77.9 1.4 copy.465
  79.2 1.5 concatenate.174
  80.7 2.0 %fusion.12 = bf16[2592,64]{0,1:T(8,128)(2,1)} fusion(bf16[12,2592]{1,0:T(8,128)(2,1)} %concatenate.174, bf16[64,12]{0,1:T(8,128)(2,1)} %param.10, f32[64]{0:T(128)} %param.11), kind=kOutput, calls=%fused_computation.18 | convolution fusion | flops 4313088 | bytes 395776 | tf_op jit(solution)/shard_map/dot_general | solution.py:48
  82.7 2.6 %fusion.7 = f32[144,2592]{1,0:T(8,128)} fusion(bf16[144,64]{0,1:T(8,128)(2,1)S(1)} %copy-done, bf16[64,64]{1,0:T(8,128)(2,1)} %param.12, bf16[2592,64]{0,1:T(8,128)(2,1)} %fusion.12, f32[144]{0:T(256)} %param.15, f32[144]{0:T(256)} %copy-done.67, f32[144]{0:T(256)} %copy-done.70, f32[64]{0:T(128)} %param.13), kind=kOutput, calls=%fused_computation.9 | convolution fusion | flops 70460928 | bytes 1853376 | tf_op jit(solution)/shard_map/dot_general | solution.py:54
  85.4 1.7 fusion.94
  87.1 1.7 fusion.93
  88.8 2.5 %slice_bitcast_fusion = (f32[18,8,8,128]{3,1,2,0:T(8,128)}, f32[18,8,8,128]{3,1,2,0:T(8,128)}) fusion(f32[144,2592]{1,0:T(8,128)} %fusion.7), kind=kLoop, calls=%fused_computation.108 | loop fusion | bytes 2359296
  95.3 1.4 convert_reduce_fusion.1
  99.3 0.9 fusion.109
  102.1 1.7 reshape.160
  103.8 1.7 reshape.161
  105.5 1.7 concatenate.182
  107.2 1.6 concatenate.184
  108.8 1.3 copy.519
  110.1 1.2 copy.522
  114.1 2.1 %collective-permute-start.13 = (f32[12,1,8,128]{3,2,1,0:T(8,128)S(1)}, f32[12,1,8,128]{3,2,1,0:T(8,128)S(1)}, u32[]{:S(2)}, u32[]{:S(2)}) collective-permute-start(f32[12,1,8,128]{3,2,1,0:T(8,128)S(1)} %get-tuple-element.80), channel_id=1, source_target_pairs={{8,0},{16,8},{24,16},{0,24},{9,1},{17,9},{25,17},{1,25},{10,2},{18... | collective-permute-start | bytes 147464 | tf_op jit(solution)/shard_map/ppermute | solution.py:22
  116.4 1.9 %collective-permute-done.13 = f32[12,1,8,128]{3,2,1,0:T(8,128)S(1)} collective-permute-done((f32[12,1,8,128]{3,2,1,0:T(8,128)S(1)}, f32[12,1,8,128]{3,2,1,0:T(8,128)S(1)}, u32[]{:S(2)}, u32[]{:S(2)}) %collective-permute-start.13) | collective-permute-done | bytes 49184 | tf_op jit(solution)/shard_map/ppermute | solution.py:22
  118.2 2.0 %collective-permute-done.12 = f32[12,1,8,128]{3,2,1,0:T(8,128)S(1)} collective-permute-done((f32[12,1,8,128]{3,2,1,0:T(8,128)S(1)}, f32[12,1,8,128]{3,2,1,0:T(8,128)S(1)}, u32[]{:S(2)}, u32[]{:S(2)}) %collective-permute-start.12) | collective-permute-done | bytes 49184 | tf_op jit(solution)/shard_map/ppermute | solution.py:21
  120.4 1.6 collective-permute-start.14
  123.0 1.4 collective-permute-done.14
  124.5 1.4 collective-permute-done.15
  126.2 1.7 collective-permute-start.17
  129.6 3.6 %collective-permute-done.16 = f32[12,4,10,1]{3,1,2,0:T(4,128)S(1)} collective-permute-done((f32[12,4,10,1]{3,1,2,0:T(4,128)S(1)}, f32[12,4,10,1]{3,1,2,0:T(4,128)S(1)}, u32[]{:S(2)}, u32[]{:S(2)}) %collective-permute-start.16) | collective-permute-done | bytes 1952 | tf_op jit(solution)/shard_map/ppermute | solution.py:21
  139.0 42.9 %all-reduce = (f32[64,12]{0,1:T(8,128)S(1)}, f32[64]{0:T(128)S(1)}, f32[64,64]{1,0:T(8,128)S(1)}, f32[64]{0:T(128)S(1)}, f32[144,64]{0,1:T(8,128)S(1)}, /*index=5*/f32[144]{0:T(256)S(1)}) all-reduce(f32[64,12]{0,1:T(8,128)S(1)} %convolution_add_fusion.14, f32[64]{0:T(128)S(1)} %add.396, ...), channel_id=1, replica_groups=mesh['gx'=4,'gy'=2,'gz'=4] {'gx','gy','gz'}, use_global_device_ids=true, to_apply=%region_9.10 | all-reduce | flops 14352 | bytes 114816 | tf_op jit(solution)/shard_map/psum | solution.py:215
  (314 shorter events, 53.1 us)
Async XLA Ops:
  0.6 13.3 %copy-start = (bf16[144,64]{0,1:T(8,128)(2,1)S(1)}, bf16[144,64]{0,1:T(8,128)(2,1)}, u32[]{:S(2)}) copy-start(bf16[144,64]{0,1:T(8,128)(2,1)} %param.14) | copy-start | bytes 55300
  0.6 13.3 %copy-start.72 = (f32[144]{0:T(256)S(1)}, f32[144]{0:T(256)}, u32[]{:S(2)}) copy-start(f32[144]{0:T(256)} %param.15) | copy-start | bytes 1732
  1.5 7.7 %collective-permute-start.1 = (f32[12,1,8,128]{3,2,1,0:T(8,128)S(1)}, f32[12,1,8,128]{3,2,1,0:T(8,128)S(1)}, u32[]{:S(2)}, u32[]{:S(2)}) collective-permute-start(f32[12,1,8,128]{3,2,1,0:T(8,128)S(1)} %get-tuple-element.83), channel_id=1, source_target_pairs={{8,0},{16,8},{24,16},{0,24},{9,1},{17,9},{25,17},{1,25},{10,2},{18... | collective-permute-start | bytes 147464 | tf_op jit(solution)/shard_map/ppermute | solution.py:22
  2.0 6.2 %collective-permute-start = (f32[12,1,8,128]{3,2,1,0:T(8,128)S(1)}, f32[12,1,8,128]{3,2,1,0:T(8,128)S(1)}, u32[]{:S(2)}, u32[]{:S(2)}) collective-permute-start(f32[12,1,8,128]{3,2,1,0:T(8,128)S(1)} %get-tuple-element.84), channel_id=1, source_target_pairs={{0,8},{8,16},{16,24},{24,0},{1,9},{9,17},{17,25},{25,1},{2,10},{10... | collective-permute-start | bytes 147464 | tf_op jit(solution)/shard_map/ppermute | solution.py:21
  3.6 26.1 %copy-start.67 = (f32[144]{0:T(256)}, f32[144]{0:T(256)S(1)}, u32[]{:S(2)}) copy-start(f32[144]{0:T(256)S(1)} %get-tuple-element.98) | copy-start | bytes 1732
  3.6 26.1 %copy-start.70 = (f32[144]{0:T(256)}, f32[144]{0:T(256)S(1)}, u32[]{:S(2)}) copy-start(f32[144]{0:T(256)S(1)} %get-tuple-element.99) | copy-start | bytes 1732
  9.3 6.1 %collective-permute-start.3 = (f32[12,4,1,128]{3,2,1,0:T(1,128)S(1)}, f32[12,4,1,128]{3,2,1,0:T(1,128)S(1)}, u32[]{:S(2)}, u32[]{:S(2)}) collective-permute-start(f32[12,4,1,128]{3,2,1,0:T(1,128)S(1)} %get-tuple-element.78), channel_id=1, source_target_pairs={{4,0},{0,4},{5,1},{1,5},{6,2},{2,6},{7,3},{3,7},{12,8},{8,12},{13,... | collective-permute-start | bytes 73736 | tf_op jit(solution)/shard_map/ppermute | solution.py:22
  9.8 5.5 %collective-permute-start.2 = (f32[12,4,1,128]{3,2,1,0:T(1,128)S(1)}, f32[12,4,1,128]{3,2,1,0:T(1,128)S(1)}, u32[]{:S(2)}, u32[]{:S(2)}) collective-permute-start(f32[12,4,1,128]{3,2,1,0:T(1,128)S(1)} %get-tuple-element.77), channel_id=1, source_target_pairs={{0,4},{4,0},{1,5},{5,1},{2,6},{6,2},{3,7},{7,3},{8,12},{12,8},{9,1... | collective-permute-start | bytes 73736 | tf_op jit(solution)/shard_map/ppermute | solution.py:21
  15.3 13.3 %copy-start.63 = (bf16[64,12]{0,1:T(8,128)(2,1)S(1)}, bf16[64,12]{0,1:T(8,128)(2,1)}, u32[]{:S(2)}) copy-start(bf16[64,12]{0,1:T(8,128)(2,1)} %param.10) | copy-start | bytes 4612
  15.3 13.3 %copy-start.76 = (f32[64]{0:T(128)S(1)}, f32[64]{0:T(128)}, u32[]{:S(2)}) copy-start(f32[64]{0:T(128)} %param.11) | copy-start | bytes 772
  15.3 14.4 %copy-start.60 = (bf16[64,64]{1,0:T(8,128)(2,1)S(1)}, bf16[64,64]{1,0:T(8,128)(2,1)}, u32[]{:S(2)}) copy-start(bf16[64,64]{1,0:T(8,128)(2,1)} %param.12) | copy-start | bytes 24580
  15.3 14.4 %copy-start.75 = (f32[64]{0:T(128)S(1)}, f32[64]{0:T(128)}, u32[]{:S(2)}) copy-start(f32[64]{0:T(128)} %param.13) | copy-start | bytes 772
  15.6 12.6 %collective-permute-start.5 = (f32[12,4,10,1]{3,2,1,0:T(8,128)S(1)}, f32[12,4,10,1]{3,2,1,0:T(8,128)S(1)}, u32[]{:S(2)}, u32[]{:S(2)}) collective-permute-start(f32[12,4,10,1]{3,2,1,0:T(8,128)S(1)} %get-tuple-element.64), channel_id=1, source_target_pairs={{1,0},{2,1},{3,2},{0,3},{5,4},{6,5},{7,6},{4,7},{9,8},{10,9},{11,1... | collective-permute-start | bytes 5768 | tf_op jit(solution)/shard_map/ppermute | solution.py:22
  15.7 11.5 %collective-permute-start.4 = (f32[12,4,10,1]{3,2,1,0:T(8,128)S(1)}, f32[12,4,10,1]{3,2,1,0:T(8,128)S(1)}, u32[]{:S(2)}, u32[]{:S(2)}) collective-permute-start(f32[12,4,10,1]{3,2,1,0:T(8,128)S(1)} %get-tuple-element.63), channel_id=1, source_target_pairs={{0,1},{1,2},{2,3},{3,0},{4,5},{5,6},{6,7},{7,4},{8,9},{9,10},{10,1... | collective-permute-start | bytes 5768 | tf_op jit(solution)/shard_map/ppermute | solution.py:21
  28.2 3.0 %copy-start.49 = (f32[12,4,10,1]{3,2,1,0:T(8,128)}, f32[12,4,10,1]{3,2,1,0:T(8,128)S(1)}, u32[]{:S(2)}) copy-start(f32[12,4,10,1]{3,2,1,0:T(8,128)S(1)} %collective-permute-done.5) | copy-start | bytes 5764
  38.1 4.4 %copy-start.3 = (f32[12,12,2,8,1]{4,3,2,1,0:T(8,128)}, f32[12,12,2,8,1]{4,3,2,1,0:T(8,128)S(1)}, u32[]{:S(2)}) copy-start(f32[12,12,2,8,1]{4,3,2,1,0:T(8,128)S(1)} %reshape.159) | copy-start | bytes 27652
  39.9 4.4 %copy-start.25 = (f32[12,12,2,1,128]{4,2,1,0,3:T(2,128)}, f32[12,12,2,1,128]{4,2,1,0,3:T(2,128)S(1)}, u32[]{:S(2)}) copy-start(f32[12,12,2,1,128]{4,2,1,0,3:T(2,128)S(1)} %concatenate.165) | copy-start | bytes 442372
  40.0 4.4 %copy-start.27 = (f32[12,12,2,1,128]{4,2,1,0,3:T(2,128)}, f32[12,12,2,1,128]{4,2,1,0,3:T(2,128)S(1)}, u32[]{:S(2)}) copy-start(f32[12,12,2,1,128]{4,2,1,0,3:T(2,128)S(1)} %concatenate.163) | copy-start | bytes 442372
  45.8 3.9 %copy-start.61 = (bf16[64,64]{1,0:T(8,128)(2,1)S(1)}, bf16[64,64]{1,0:T(8,128)(2,1)}, u32[]{:S(2)}) copy-start(bf16[64,64]{1,0:T(8,128)(2,1)} %param.12) | copy-start | bytes 24580
  46.0 6.9 %copy-start.56 = (bf16[2,8,16,128]{3,1,2,0:T(8,128)(2,1)}, bf16[2,8,16,128]{3,1,2,0:T(8,128)(2,1)S(1)}, u32[]{:S(2)}) copy-start(bf16[2,8,16,128]{3,1,2,0:T(8,128)(2,1)S(1)} %copy.520) | copy-start | bytes 196612
  46.3 6.6 %copy-start.29 = (bf16[2048,64]{0,1:T(8,128)(2,1)}, bf16[2048,64]{0,1:T(8,128)(2,1)S(1)}, u32[]{:S(2)}) copy-start(bf16[2048,64]{0,1:T(8,128)(2,1)S(1)} %fusion.28) | copy-start | bytes 786436
  46.3 6.5 %collective-permute-start.7 = (f32[24,1,8,128]{3,2,1,0:T(8,128)S(1)}, f32[24,1,8,128]{3,2,1,0:T(8,128)S(1)}, u32[]{:S(2)}, u32[]{:S(2)}) collective-permute-start(f32[24,1,8,128]{3,2,1,0:T(8,128)S(1)} %get-tuple-element.76), channel_id=1, source_target_pairs={{8,0},{16,8},{24,16},{0,24},{9,1},{17,9},{25,17},{1,25},{10,2},{18... | collective-permute-start | bytes 294920 | tf_op jit(solution)/shard_map/ppermute | solution.py:22
  49.7 4.6 %collective-permute-start.6 = (f32[24,1,8,128]{3,2,1,0:T(8,128)S(1)}, f32[24,1,8,128]{3,2,1,0:T(8,128)S(1)}, u32[]{:S(2)}, u32[]{:S(2)}) collective-permute-start(f32[24,1,8,128]{3,2,1,0:T(8,128)S(1)} %get-tuple-element.75), channel_id=1, source_target_pairs={{0,8},{8,16},{16,24},{24,0},{1,9},{9,17},{17,25},{25,1},{2,10},{10... | collective-permute-start | bytes 294920 | tf_op jit(solution)/shard_map/ppermute | solution.py:21
  52.9 6.2 %copy-start.17 = (f32[24,1,8,128]{3,2,1,0:T(8,128)}, f32[24,1,8,128]{3,2,1,0:T(8,128)S(1)}, u32[]{:S(2)}) copy-start(f32[24,1,8,128]{3,2,1,0:T(8,128)S(1)} %collective-permute-done.7) | copy-start | bytes 294916
  54.3 4.8 %copy-start.19 = (f32[24,1,8,128]{3,2,1,0:T(8,128)}, f32[24,1,8,128]{3,2,1,0:T(8,128)S(1)}, u32[]{:S(2)}) copy-start(f32[24,1,8,128]{3,2,1,0:T(8,128)S(1)} %collective-permute-done.6) | copy-start | bytes 294916
  54.4 4.5 %collective-permute-start.9 = (f32[24,4,1,128]{3,2,1,0:T(1,128)S(1)}, f32[24,4,1,128]{3,2,1,0:T(1,128)S(1)}, u32[]{:S(2)}, u32[]{:S(2)}) collective-permute-start(f32[24,4,1,128]{3,2,1,0:T(1,128)S(1)} %get-tuple-element.62), channel_id=1, source_target_pairs={{4,0},{0,4},{5,1},{1,5},{6,2},{2,6},{7,3},{3,7},{12,8},{8,12},{13,... | collective-permute-start | bytes 147464 | tf_op jit(solution)/shard_map/ppermute | solution.py:22
  55.0 4.1 %collective-permute-start.8 = (f32[24,4,1,128]{3,2,1,0:T(1,128)S(1)}, f32[24,4,1,128]{3,2,1,0:T(1,128)S(1)}, u32[]{:S(2)}, u32[]{:S(2)}) collective-permute-start(f32[24,4,1,128]{3,2,1,0:T(1,128)S(1)} %get-tuple-element.61), channel_id=1, source_target_pairs={{0,4},{4,0},{1,5},{5,1},{2,6},{6,2},{3,7},{7,3},{8,12},{12,8},{9,1... | collective-permute-start | bytes 147464 | tf_op jit(solution)/shard_map/ppermute | solution.py:21
  61.2 6.5 %collective-permute-start.11 = (f32[24,4,10,1]{0,1,3,2:T(4,128)}, f32[24,4,10,1]{0,1,3,2:T(4,128)S(1)}, u32[]{:S(2)}, u32[]{:S(2)}) collective-permute-start(f32[24,4,10,1]{0,1,3,2:T(4,128)} %copy.462), channel_id=1, source_target_pairs={{1,0},{2,1},{3,2},{0,3},{5,4},{6,5},{7,6},{4,7},{9,8},{10,9},{11,1... | collective-permute-start | bytes 11528 | tf_op jit(solution)/shard_map/ppermute | solution.py:22
  61.6 6.8 %collective-permute-start.10 = (f32[24,4,10,1]{0,1,3,2:T(4,128)S(1)}, f32[24,4,10,1]{0,1,3,2:T(4,128)}, u32[]{:S(2)}, u32[]{:S(2)}) collective-permute-start(f32[24,4,10,1]{0,1,3,2:T(4,128)S(1)} %copy.460), channel_id=1, source_target_pairs={{0,1},{1,2},{2,3},{3,0},{4,5},{5,6},{6,7},{7,4},{8,9},{9,10},{10,1... | collective-permute-start | bytes 11528 | tf_op jit(solution)/shard_map/ppermute | solution.py:21
  85.3 5.9 %copy-start.10 = (f32[12,2,8,128]{3,2,1,0:T(8,128)S(1)}, f32[12,2,8,128]{3,2,1,0:T(8,128)}, u32[]{:S(2)}) copy-start(f32[12,2,8,128]{3,2,1,0:T(8,128)} %param.9) | copy-start | bytes 294916
  85.3 5.9 %copy-start.18 = (f32[24,1,8,128]{3,2,1,0:T(8,128)S(1)}, f32[24,1,8,128]{3,2,1,0:T(8,128)}, u32[]{:S(2)}) copy-start(f32[24,1,8,128]{3,2,1,0:T(8,128)} %copy-done.17) | copy-start | bytes 294916
  85.3 5.9 %copy-start.20 = (f32[24,1,8,128]{3,2,1,0:T(8,128)S(1)}, f32[24,1,8,128]{3,2,1,0:T(8,128)}, u32[]{:S(2)}) copy-start(f32[24,1,8,128]{3,2,1,0:T(8,128)} %copy-done.19) | copy-start | bytes 294916
  85.4 5.9 %copy-start.32 = (f32[24,4,1,128]{3,2,1,0:T(1,128)S(1)}, f32[24,4,1,128]{3,2,1,0:T(1,128)}, u32[]{:S(2)}) copy-start(f32[24,4,1,128]{3,2,1,0:T(1,128)} %copy-done.31) | copy-start | bytes 147460
  96.7 3.5 %copy-start.64 = (bf16[64,12]{0,1:T(8,128)(2,1)S(1)}, bf16[64,12]{0,1:T(8,128)(2,1)}, u32[]{:S(2)}) copy-start(bf16[64,12]{0,1:T(8,128)(2,1)} %param.10) | copy-start | bytes 4612
  97.5 3.5 %copy-start.71 = (f32[144]{0:T(256)S(1)}, f32[144]{0:T(256)}, u32[]{:S(2)}) copy-start(f32[144]{0:T(256)} %copy-done.70) | copy-start | bytes 1732
  101.3 2.6 %copy-start.52 = (f32[144,16]{1,0:T(8,128)S(1)}, f32[144,16]{1,0:T(8,128)}, u32[]{:S(2)}) copy-start(f32[144,16]{1,0:T(8,128)} %get-tuple-element.47) | copy-start | bytes 27652
  105.5 5.8 %copy-start.34 = (f32[12,2,8,129]{3,2,1,0:T(8,128)S(1)}, f32[12,2,8,129]{3,2,1,0:T(8,128)}, u32[]{:S(2)}) copy-start(f32[12,2,8,129]{3,2,1,0:T(8,128)} %get-tuple-element.33) | copy-start | bytes 297220
  113.1 3.1 %copy-start.57 = (bf16[2,8,16,128]{3,1,2,0:T(8,128)(2,1)S(1)}, bf16[2,8,16,128]{3,1,2,0:T(8,128)(2,1)}, u32[]{:S(2)}) copy-start(bf16[2,8,16,128]{3,1,2,0:T(8,128)(2,1)} %copy-done.56) | copy-start | bytes 196612
  113.3 9.2 %copy-start.43 = (f32[12,3,8,128]{3,2,1,0:T(8,128)S(1)}, f32[12,3,8,128]{3,2,1,0:T(8,128)}, u32[]{:S(2)}) copy-start(f32[12,3,8,128]{3,2,1,0:T(8,128)} %get-tuple-element.38) | copy-start | bytes 442372
  114.1 4.1 %collective-permute-start.13 = (f32[12,1,8,128]{3,2,1,0:T(8,128)S(1)}, f32[12,1,8,128]{3,2,1,0:T(8,128)S(1)}, u32[]{:S(2)}, u32[]{:S(2)}) collective-permute-start(f32[12,1,8,128]{3,2,1,0:T(8,128)S(1)} %get-tuple-element.80), channel_id=1, source_target_pairs={{8,0},{16,8},{24,16},{0,24},{9,1},{17,9},{25,17},{1,25},{10,2},{18... | collective-permute-start | bytes 147464 | tf_op jit(solution)/shard_map/ppermute | solution.py:22
  116.2 4.1 %collective-permute-start.12 = (f32[12,1,8,128]{3,2,1,0:T(8,128)S(1)}, f32[12,1,8,128]{3,2,1,0:T(8,128)S(1)}, u32[]{:S(2)}, u32[]{:S(2)}) collective-permute-start(f32[12,1,8,128]{3,2,1,0:T(8,128)S(1)} %get-tuple-element.79), channel_id=1, source_target_pairs={{0,8},{8,16},{16,24},{24,0},{1,9},{9,17},{17,25},{25,1},{2,10},{10... | collective-permute-start | bytes 147464 | tf_op jit(solution)/shard_map/ppermute | solution.py:21
  120.4 4.0 %collective-permute-start.14 = (f32[12,4,1,128]{3,0,2,1:T(8,128)S(1)}, f32[12,4,1,128]{3,0,2,1:T(8,128)S(1)}, u32[]{:S(2)}, u32[]{:S(2)}) collective-permute-start(f32[12,4,1,128]{3,0,2,1:T(8,128)S(1)} %get-tuple-element.68), channel_id=1, source_target_pairs={{0,4},{4,0},{1,5},{5,1},{2,6},{6,2},{3,7},{7,3},{8,12},{12,8},{9,1... | collective-permute-start | bytes 73736 | tf_op jit(solution)/shard_map/ppermute | solution.py:21
  122.0 3.9 %collective-permute-start.15 = (f32[12,4,1,128]{3,0,2,1:T(8,128)S(1)}, f32[12,4,1,128]{3,0,2,1:T(8,128)S(1)}, u32[]{:S(2)}, u32[]{:S(2)}) collective-permute-start(f32[12,4,1,128]{3,0,2,1:T(8,128)S(1)} %get-tuple-element.67), channel_id=1, source_target_pairs={{4,0},{0,4},{5,1},{1,5},{6,2},{2,6},{7,3},{3,7},{12,8},{8,12},{13,... | collective-permute-start | bytes 73736 | tf_op jit(solution)/shard_map/ppermute | solution.py:22
  123.0 5.1 %copy-start.36 = (f32[12,2,9,128]{3,2,1,0:T(8,128)S(1)}, f32[12,2,9,128]{3,2,1,0:T(8,128)}, u32[]{:S(2)}) copy-start(f32[12,2,9,128]{3,2,1,0:T(8,128)} %get-tuple-element.40) | copy-start | bytes 331780
  126.1 7.0 %collective-permute-start.16 = (f32[12,4,10,1]{3,1,2,0:T(4,128)S(1)}, f32[12,4,10,1]{3,1,2,0:T(4,128)S(1)}, u32[]{:S(2)}, u32[]{:S(2)}) collective-permute-start(f32[12,4,10,1]{3,1,2,0:T(4,128)S(1)} %get-tuple-element.71), channel_id=1, source_target_pairs={{0,1},{1,2},{2,3},{3,0},{4,5},{5,6},{6,7},{7,4},{8,9},{9,10},{10,1... | collective-permute-start | bytes 5768 | tf_op jit(solution)/shard_map/ppermute | solution.py:21
  126.2 7.0 %collective-permute-start.17 = (f32[12,4,10,1]{3,1,2,0:T(4,128)S(1)}, f32[12,4,10,1]{3,1,2,0:T(4,128)S(1)}, u32[]{:S(2)}, u32[]{:S(2)}) collective-permute-start(f32[12,4,10,1]{3,1,2,0:T(4,128)S(1)} %get-tuple-element.72), channel_id=1, source_target_pairs={{1,0},{2,1},{3,2},{0,3},{5,4},{6,5},{7,6},{4,7},{9,8},{10,9},{11,1... | collective-permute-start | bytes 5768 | tf_op jit(solution)/shard_map/ppermute | solution.py:22
  129.0 4.6 %copy-start.35 = (f32[12,2,8,129]{3,2,1,0:T(8,128)S(1)}, f32[12,2,8,129]{3,2,1,0:T(8,128)}, u32[]{:S(2)}) copy-start(f32[12,2,8,129]{3,2,1,0:T(8,128)} %get-tuple-element.42) | copy-start | bytes 297220
  138.2 47.2 %copy-start.24 = (f32[12,2,8,128]{3,2,1,0:T(8,128)S(1)}, f32[12,2,8,128]{3,2,1,0:T(8,128)}, u32[]{:S(2)}) copy-start(f32[12,2,8,128]{3,2,1,0:T(8,128)} %param.8) | copy-start | bytes 294916
  (50 other events, 61.2 us)
where the time goes:
time: 188 us; the launch traced here: 186 us
  local copies, waits for them, and re-layouts  51.3 us (27%)
  blocking collectives  42.9 us (23%)
  waiting for transfers between devices  29.6 us (16%)
  other arithmetic  26.2 us (14%)
  matrix products  17.5 us (9%)
  starting transfers between devices  16.8 us (9%)
    psum x1, blocking collectives, shards(): lax.psum((grads_late[0], grads_late[1], grads_late[2], grads_late[3], gra...  42.9 us
    ppermute x9, waiting for transfers between devices, extended_2(): before = lax.ppermute(last, axis, up)  24 us
    unnamed x196, local copies, waits for them, and re-layouts  21.9 us
    ppermute x9, starting transfers between devices, extended_2(): after = lax.ppermute(leading, axis, down)  9.38 us
    concatenate x8, local copies, waits for them, and re-layouts, joined(): jnp.concatenate([jnp.expand_dims(lower_slab, spatial), inner_mob, jnp.exp...  9.13 us
    ppermute x9, starting transfers between devices, extended_2(): before = lax.ppermute(last, axis, up)  7.46 us
    dot_general x4, matrix products, forward_net(): jnp.dot(weight_three, hidden_two, preferred_element_type=jnp.float32)  5.89 us
    ppermute x9, waiting for transfers between devices, extended_2(): after = lax.ppermute(leading, axis, down)  5.53 us
  transfers between devices with their start and end apart: 18, of which 10 were waited for; matrix products, arithmetic and copies ran while one was open for 8% of the time, Pallas kernels for 0%

commit v1 on v0

v1 whole, which is shorter than its diff:
```python
import functools
import math

import jax
import jax.numpy as jnp
from jax import lax
from jax.experimental import pallas as pl
from jax.experimental.pallas import tpu as pltpu
from jax.sharding import PartitionSpec as P

step_size = 0.08
cubic_coef = 0.1
diag_scale = 0.5
off_scale = 0.04
axes = ("gx", "gy", "gz")
F32 = jnp.float32
BF16 = jnp.bfloat16


def potential(v):
    return v + cubic_coef * v * v * v


def iota(shape, dim):
    return lax.broadcasted_iota(jnp.int32, shape, dim)


def dot(a, b):
    return jnp.dot(a, b, preferred_element_type=F32)


def dot_nt(a, b):
    return lax.dot_general(a, b, (((1,), (1,)), ((), ())), preferred_element_type=F32)


def split_two(v):
    high = v.astype(BF16)
    return high, (v - high.astype(F32)).astype(BF16)


def rolled(v, shift, axis):
    shift = shift % v.shape[axis]
    return pltpu.roll(v, shift, axis) if shift else v


def log2(n):
    assert n & (n - 1) == 0
    return n.bit_length() - 1


def kernel(
    dims, comp, cot, w1, b1, w2, b2, w3, b3, out, pay,
    vec, ybuf, zbuf, xhalo, yhalo, zhalo,
    w1x, w1t, w2x, w2t, w3x, w3t, e3, bb1, bb2, bb3,
    xin, hid1, hid2, act, arim, dpot, dcot, drim, tin, trim, pack, p3, r1, r2, r3, q1, q2, q3,
    send_sem, recv_sem,
):
    nc, nx, ny, nz, h1, h2 = dims
    width = nx * nz
    mm = nc * nc
    sy = log2(ny)
    grp = 256 // h1

    here = {a: lax.axis_index(a) for a in axes}
    size = {a: lax.axis_size(a) for a in axes}
    up = {a: {a: lax.rem(here[a] + 1, size[a])} for a in axes}
    down = {a: {a: lax.rem(here[a] + size[a] - 1, size[a])} for a in axes}
    barrier = pltpu.get_barrier_semaphore()
    for a in axes:
        for target in (up[a], down[a]):
            pl.semaphore_signal(barrier, inc=1, device_id=target, device_id_type=pl.DeviceIdType.MESH)

    lane3 = iota((nc, ny, nz), 2)
    row3 = iota((nc, ny, nz), 1)
    lane2 = iota((ny, nz), 1)

    def planes(v):
        return [v[:, :, x * nz : (x + 1) * nz] for x in range(nx)]

    def own_ends(v):
        total = jnp.zeros((nc, ny, nz), F32)
        for x, plane in enumerate(planes(v)):
            total = jnp.where(lane3 == x, rolled(plane, x, 2), total)
            total = jnp.where(lane3 == nx + x, rolled(plane, nx + x + 1, 2), total)
        return total

    def fill(e):
        for c in range(nc):
            for x in range(nx):
                cols = slice(x * nz, (x + 1) * nz)
                ybuf[e, 0, c * nx + x : c * nx + x + 1, :] = vec[e, c, 0:1, cols]
                ybuf[e, 1, c * nx + x : c * nx + x + 1, :] = vec[e, c, ny - 1 : ny, cols]
        ends = own_ends(vec[e])
        total = ends[0]
        for c in range(1, nc):
            total = total + rolled(ends[c], c * 2 * nx, 1)
        zbuf[e] = total

    def copies(e):
        moves = (
            (vec.at[e, :, :, width - nz : width], xhalo.at[e, 0], up["gx"]),
            (vec.at[e, :, :, 0:nz], xhalo.at[e, 1], down["gx"]),
            (ybuf.at[e, 1], yhalo.at[e, 0], up["gy"]),
            (ybuf.at[e, 0], yhalo.at[e, 1], down["gy"]),
            (zbuf.at[e], zhalo.at[e, 0], up["gz"]),
            (zbuf.at[e], zhalo.at[e, 1], down["gz"]),
        )
        return [
            pltpu.make_async_remote_copy(
                src_ref=src, dst_ref=dst, send_sem=send_sem.at[e, k], recv_sem=recv_sem.at[e, k],
                device_id=target, device_id_type=pl.DeviceIdType.MESH,
            )
            for k, (src, dst, target) in enumerate(moves)
        ]

    def start(e):
        for copy in copies(e):
            copy.start()

    def finish(e):
        for copy in copies(e):
            copy.wait()

    def received_ends(e):
        phase = lane2 & (2 * nx - 1)
        low = jnp.where(phase < nx, rolled(zhalo[e, 0], -nx, 1), 0.0)
        high = jnp.where(phase >= nx, rolled(zhalo[e, 1], nx, 1), 0.0)
        total = low + high
        return jnp.stack([rolled(total, -c * 2 * nx, 1) for c in range(nc)], axis=0)

    def packed(low, high, ends):
        for c in range(nc):
            pack[c, 0:nx, :] = low[c * nx : (c + 1) * nx, :]
            pack[c, nx : 2 * nx, :] = high[c * nx : (c + 1) * nx, :]
        half = ny // 2
        folded = jnp.where(lane3 < 2 * nx, rolled(ends, half, 1), rolled(ends, 2 * nx, 2))
        folded = jnp.where(lane3 < 4 * nx, folded, 0.0)
        return jnp.where(row3 < half, pack[...], folded)

    def neighbours(v, low_x, high_x, rim, ends):
        parts = planes(v)
        x_low = jnp.concatenate([low_x] + parts[:-1], axis=2)
        x_high = jnp.concatenate(parts[1:] + [high_x], axis=2)
        found = [[], [], [], []]
        for x, plane in enumerate(parts):
            found[0].append(jnp.where(row3 == 0, rim[:, x : x + 1, :], rolled(plane, 1, 1)))
            found[1].append(
                jnp.where(row3 == ny - 1, rim[:, nx + x : nx + x + 1, :], rolled(plane, -1, 1))
            )
            found[2].append(jnp.where(lane3 == 0, rolled(ends, -x, 2), rolled(plane, 1, 2)))
            found[3].append(
                jnp.where(lane3 == nz - 1, rolled(ends, nz - 1 - nx - x, 2), rolled(plane, -1, 2))
            )
        return [x_low, x_high] + [jnp.concatenate(f, axis=2) for f in found]

    def halo(e):
        ends = received_ends(e)
        rim = packed(yhalo[e, 0], yhalo[e, 1], ends)
        return xhalo[e, 0], xhalo[e, 1], rim, ends

    def differences(e, inner, low_x, high_x, rim, ends, mapping, target, which):
        v = mapping(inner)
        lx, hx, mrim = mapping(low_x), mapping(high_x), mapping(rim)
        for d, other in enumerate(neighbours(v, lx, hx, mrim, mapping(ends))):
            target[d] = v - other
        own = mapping(packed(ybuf[e, 0], ybuf[e, 1], own_ends(inner)))
        drim[which] = jnp.concatenate(
            [lx - v[:, :, 0:nz], hx - v[:, :, width - nz : width], mrim - own], axis=2
        )

    def net(v, target, keep):
        lanes = v.shape[2]

        def wide(ref):
            return jnp.concatenate([ref[...]] * (lanes // 128), axis=1)

        flat = v.reshape(nc * ny, lanes).astype(BF16)
        one = jnp.tanh(dot(w1x[...], flat) + wide(bb1)).astype(BF16)
        bias = wide(bb2)
        two = []
        span = grp * h1
        for g in range(ny // grp):
            rows = slice(g * span, (g + 1) * span)
            two.append(jnp.tanh(dot(w2x[...], one[rows]) + bias[rows]).astype(BF16))
        two = jnp.concatenate(two, axis=0)
        target[...] = jnp.tanh(dot(w3x[...], two) + wide(bb3))
        if keep is not None:
            xin[keep] = flat
            hid1[keep] = one
            hid2[keep] = two

    def apply(a_ref, d_ref, t_ref, count, transposed):
        def body(k, carry):
            sums = [None] * count
            for q in range(nc):
                at = (q * nc + k) * ny if transposed else (k * nc + q) * ny
                m = a_ref[pl.ds(pl.multiple_of(at, ny), ny), :]
                for d in range(count):
                    term = m * d_ref[d, q]
                    sums[d] = term if sums[d] is None else sums[d] + term
            at = pl.multiple_of(k * (nc + 1) * ny, ny)
            own = 1.0 + (diag_scale - off_scale) * a_ref[pl.ds(at, ny), :]
            for d in range(count):
                t_ref[d, k] = d_ref[d, k] * own + off_scale * sums[d]
            return carry

        lax.fori_loop(0, nc, body, 0)

    def inner_flow(s, d_ref, transposed):
        apply(act.at[s], d_ref, tin, 6, transposed)
        total = -(tin[0] + tin[1] + tin[2] + tin[3] + tin[4] + tin[5])
        zero = jnp.zeros((nc, ny, nz), F32)
        low, high = planes(tin[0]), planes(tin[1])
        total = total + jnp.concatenate(low[1:] + [zero], axis=2)
        total = total + jnp.concatenate([zero] + high[:-1], axis=2)
        moved = []
        for x in range(nx):
            cols = slice(x * nz, (x + 1) * nz)
            to_low_y = jnp.where(row3 == ny - 1, 0.0, rolled(tin[2, :, :, cols], -1, 1))
            to_high_y = jnp.where(row3 == 0, 0.0, rolled(tin[3, :, :, cols], 1, 1))
            to_low_z = jnp.where(lane3 == nz - 1, 0.0, rolled(tin[4, :, :, cols], -1, 2))
            to_high_z = jnp.where(lane3 == 0, 0.0, rolled(tin[5, :, :, cols], 1, 2))
            moved.append((to_low_y + to_high_y) + (to_low_z + to_high_z))
        return total + jnp.concatenate(moved, axis=2)

    def rim_flow(s, which, transposed):
        apply(arim.at[s], drim.at[pl.ds(which, 1)], trim, 1, transposed)
        half = ny // 2
        t = trim[0, :, :, 2 * nz : 3 * nz]
        ends = jnp.where(row3 < half, rolled(t, half, 1), rolled(t, -2 * nx, 2))
        parts = []
        for x in range(nx):
            part = jnp.where(row3 == 0, t[:, x : x + 1, :], 0.0)
            part = part + jnp.where(row3 == ny - 1, t[:, nx + x : nx + x + 1, :], 0.0)
            part = part + jnp.where(lane3 == 0, rolled(ends, -x, 2), 0.0)
            part = part + jnp.where(lane3 == nz - 1, rolled(ends, nz - 1 - nx - x, 2), 0.0)
            if x == 0:
                part = part + trim[0, :, :, 0:nz]
            if x == nx - 1:
                part = part + trim[0, :, :, nz : 2 * nz]
            parts.append(part)
        return jnp.concatenate(parts, axis=2)

    def back_net(s, first):
        def body(a, carry):
            left = [dcot[d, a] for d in range(6)]
            for b in range(0, nc, 2):
                pair = []
                for k in (b, b + 1):
                    total = left[0] * dpot[s, 0, k]
                    for d in range(1, 6):
                        total = total + left[d] * dpot[s, d, k]
                    at = pl.multiple_of((a * nc + k) * ny, ny)
                    active = act[s, pl.ds(at, ny), :]
                    scale = jnp.where(a == k, -0.5 * step_size * diag_scale, -0.5 * step_size * off_scale)
                    pair.append(total * scale * (1.0 - active * active))
                at = pl.multiple_of((a * nc + b) * ny, 2 * ny)
                p3[pl.ds(at, 2 * ny), :] = jnp.concatenate(pair, axis=0).astype(BF16)
            return carry

        lax.fori_loop(0, nc, body, 0)
        pre_three = p3[...]
        two = hid2[s]
        one = hid1[s]
        upper = two.astype(F32)
        pre_two = (dot(w3t[...], pre_three) * (1.0 - upper * upper)).astype(BF16)
        upper = one.astype(F32)
        span = grp * h1
        pre_one = []
        for g in range(ny // grp):
            rows = slice(g * span, (g + 1) * span)
            pre_one.append(
                (dot(w2t[...], pre_two[rows]) * (1.0 - upper[rows] * upper[rows])).astype(BF16)
            )
        pre_one = jnp.concatenate(pre_one, axis=0)
        net_grad = dot(w1t[...], pre_one).reshape(nc, ny, width)

        def grads():
            even = odd = None
            for y in range(0, ny, 2):
                pair = one[y * h1 : (y + 2) * h1]
                e_term = dot_nt(pre_two[y * h2 : (y + 1) * h2], pair)
                o_term = dot_nt(pre_two[(y + 1) * h2 : (y + 2) * h2], pair)
                even = e_term if even is None else even + e_term
                odd = o_term if odd is None else odd + o_term

            def over_rows(v, rows):
                v = v.astype(F32)
                total = v[0:rows]
                for y in range(1, ny):
                    total = total + v[y * rows : (y + 1) * rows]
                return total

            values = (
                (r1, dot_nt(pre_one, xin[s])),
                (r2, odd + rolled(even, h1, 1)),
                (r3, dot_nt(pre_three, two)),
                (q1, over_rows(pre_one, h1)),
                (q2, over_rows(pre_two, h2)),
                (q3, dot(e3[...], pre_three)),
            )
            for ref, value in values:
                ref[...] = value if first else ref[...] + value

        return net_grad, grads

    for x in range(nx):
        vec[0, :, :, x * nz : (x + 1) * nz] = comp[:, x]
        vec[1, :, :, x * nz : (x + 1) * nz] = cot[:, x]
    fill(0)
    fill(1)
    pl.semaphore_wait(barrier, 6)
    start(0)
    start(1)

    sh = log2(h1)
    rows_h, rows_m, rows_c = ny * h1, mm * ny, nc * ny

    def select(mask, value):
        return jnp.where(mask, value, 0.0).astype(BF16)

    def ones(mask):
        return jnp.where(mask, 1.0, 0.0).astype(BF16)

    tile = ones((iota((h1, rows_h), 1) & (h1 - 1)) == iota((h1, rows_h), 0))
    unit = ones(iota((h1, h1), 1) == iota((h1, h1), 0))
    spread_c = ones((iota((nc, rows_c), 1) >> sy) == iota((nc, rows_c), 0))
    spread_ct = ones((iota((rows_c, nc), 0) >> sy) == iota((rows_c, nc), 1))
    spread_mt = ones((iota((rows_m, mm), 0) >> sy) == iota((rows_m, mm), 1))
    e3[...] = ones((iota((mm, rows_m), 1) >> sy) == iota((mm, rows_m), 0))

    mask_hc = (iota((rows_h, rows_c), 0) >> sh) == (iota((rows_h, rows_c), 1) & (ny - 1))
    w1x[...] = select(mask_hc, jnp.concatenate([dot(w1[...], spread_c)] * ny, axis=0))
    mask_ch = (iota((rows_c, rows_h), 1) >> sh) == (iota((rows_c, rows_h), 0) & (ny - 1))
    w1t[...] = select(mask_ch, dot(dot_nt(spread_ct, w1[...]).astype(BF16), tile))
    span = grp * h1
    mask_g = (iota((span, span), 0) >> sh) == (iota((span, span), 1) >> sh)
    flipped = dot_nt(unit, w2[...]).astype(BF16)
    w2x[...] = select(mask_g, jnp.concatenate([dot(w2[...], tile[:, 0:span])] * grp, axis=0))
    w2t[...] = select(mask_g, jnp.concatenate([dot(flipped, tile[:, 0:span])] * grp, axis=0))
    mask_mh = (iota((rows_m, rows_h), 0) & (ny - 1)) == (iota((rows_m, rows_h), 1) >> sh)
    w3x[...] = select(mask_mh, dot(dot(spread_mt, w3[...]).astype(BF16), tile))
    mask_hm = (iota((rows_h, rows_m), 1) & (ny - 1)) == (iota((rows_h, rows_m), 0) >> sh)
    flipped = dot_nt(unit, w3[...]).astype(BF16)
    w3t[...] = select(mask_hm, jnp.concatenate([dot(flipped, e3[...])] * ny, axis=0))

    def column(mask, b):
        return jnp.sum(jnp.where(mask, b[...], 0.0), axis=1, keepdims=True)

    mask_b = (iota((rows_h, h1), 0) & (h1 - 1)) == iota((rows_h, h1), 1)
    bb1[...] = jnp.broadcast_to(column(mask_b, b1), bb1.shape)
    bb2[...] = jnp.broadcast_to(column(mask_b, b2), bb2.shape)
    mask_b = (iota((rows_m, mm), 0) >> sy) == iota((rows_m, mm), 1)
    bb3[...] = jnp.broadcast_to(column(mask_b, b3), bb3.shape)

    def same(v):
        return v

    net(vec[0], act.at[0], 0)
    finish(0)
    low_x, high_x, rim, ends = halo(0)
    net(jnp.concatenate([low_x, high_x, rim], axis=2), arim.at[0], None)
    differences(0, vec[0], low_x, high_x, rim, ends, potential, dpot.at[0], 0)
    vec[2] = vec[0] + 0.5 * step_size * (inner_flow(0, dpot.at[0], False) + rim_flow(0, 0, False))
    fill(2)
    start(2)

    net(vec[2], act.at[1], 1)
    finish(1)
    low_x, high_x, rim, ends = halo(1)
    differences(1, vec[1], low_x, high_x, rim, ends, same, dcot, 0)
    flow = inner_flow(1, dcot, True)
    finish(2)
    low_x, high_x, rim, ends = halo(2)
    net(jnp.concatenate([low_x, high_x, rim], axis=2), arim.at[1], None)
    differences(2, vec[2], low_x, high_x, rim, ends, potential, dpot.at[1], 1)
    flow = flow + rim_flow(1, 0, True)
    net_grad, grads = back_net(1, True)

    def slope(v):
        return 1.0 + 3.0 * cubic_coef * v * v

    vec[3] = vec[1] + 0.5 * step_size * flow * slope(vec[2]) + net_grad
    fill(3)
    start(3)
    grads()

    finish(3)
    low_x, high_x, rim, ends = halo(3)
    differences(3, vec[3], low_x, high_x, rim, ends, same, dcot, 0)
    net_grad, grads = back_net(0, False)
    grads()
    flow = inner_flow(0, dcot, True) + rim_flow(0, 0, True)
    result = vec[3] + 0.5 * step_size * flow * slope(vec[0]) + net_grad
    for x in range(nx):
        out[:, x] = result[:, :, x * nz : (x + 1) * nz]

    high, low = split_two(jnp.where(mask_mh, r3[...], 0.0))
    wide = dot(e3[...], high) + dot(e3[...], low)
    fold = wide[:, 0:128]
    for k in range(1, rows_h // 128):
        fold = fold + wide[:, k * 128 : (k + 1) * 128]
    fold = fold + rolled(fold, h1, 1)
    first = jnp.where(mask_hc, r1[...], 0.0)
    total = first[0:h1]
    for y in range(1, ny):
        total = total + first[y * h1 : (y + 1) * h1]
    place = ones(iota((rows_c, 128), 1) == h1 + (iota((rows_c, 128), 0) >> sy))
    high, low = split_two(total)
    one = dot(high, place) + dot(low, place)
    s1 = jnp.sum(q1[...], axis=1, keepdims=True)
    s2 = jnp.sum(q2[...], axis=1, keepdims=True)
    s3 = jnp.sum(q3[...], axis=1, keepdims=True)
    lane = iota((h1, 128), 1)
    at = h1 + nc
    for k, part in enumerate((s1, s2, s3[0:h1], s3[h1 : 2 * h1])):
        one = jnp.where(lane == at + k, part, one)
    pay[0:h1, :] = jnp.where(lane < h1, fold[0:h1], r2[...])
    pay[h1 : 2 * h1, :] = jnp.where(lane < h1, fold[h1 : 2 * h1], one)
    rest = mm - 2 * h1
    pay[2 * h1 : mm, :] = jnp.where(
        iota((rest, 128), 1) < h1, fold[2 * h1 : mm], s3[2 * h1 : mm]
    )


def shards(
    composition, cotangent, weight_one, bias_one, weight_two, bias_two, weight_three, bias_three
):
    nc, nx, ny, nz = composition.shape
    h1, h2 = weight_one.shape[0], weight_two.shape[0]
    mm = nc * nc
    width = nx * nz
    assert h1 == h2 and 2 * h1 == 128 and nz == 128 and 4 * nx == ny and 2 * h1 <= mm
    rows_h, rows_m, rows_c = ny * h1, mm * ny, nc * ny
    span = 256 // h1 * h1
    vmem = pltpu.VMEM
    result, pay = pl.pallas_call(
        functools.partial(kernel, (nc, nx, ny, nz, h1, h2)),
        out_shape=(
            jax.ShapeDtypeStruct(composition.shape, F32),
            jax.ShapeDtypeStruct((mm, 128), F32),
        ),
        in_specs=[pl.BlockSpec(memory_space=vmem)] * 8,
        out_specs=(pl.BlockSpec(memory_space=vmem), pl.BlockSpec(memory_space=vmem)),
        scratch_shapes=[
            vmem((4, nc, ny, width), F32),
            vmem((4, 2, nc * nx, nz), F32),
            vmem((4, ny, nz), F32),
            vmem((4, 2, nc, ny, nz), F32),
            vmem((4, 2, nc * nx, nz), F32),
            vmem((4, 2, ny, nz), F32),
            vmem((rows_h, rows_c), BF16),
            vmem((rows_c, rows_h), BF16),
            vmem((span, span), BF16),
            vmem((span, span), BF16),
            vmem((rows_m, rows_h), BF16),
            vmem((rows_h, rows_m), BF16),
            vmem((mm, rows_m), BF16),
            vmem((rows_h, 128), F32),
            vmem((rows_h, 128), F32),
            vmem((rows_m, 128), F32),
            vmem((2, rows_c, width), BF16),
            vmem((2, rows_h, width), BF16),
            vmem((2, rows_h, width), BF16),
            vmem((2, rows_m, width), F32),
            vmem((2, rows_m, 3 * nz), F32),
            vmem((2, 6, nc, ny, width), F32),
            vmem((6, nc, ny, width), F32),
            vmem((2, nc, ny, 3 * nz), F32),
            vmem((6, nc, ny, width), F32),
            vmem((1, nc, ny, 3 * nz), F32),
            vmem((nc, ny, nz), F32),
            vmem((rows_m, width), BF16),
            vmem((rows_h, rows_c), F32),
            vmem((h2, 2 * h1), F32),
            vmem((rows_m, rows_h), F32),
            vmem((h1, width), F32),
            vmem((h2, width), F32),
            vmem((mm, width), F32),
            pltpu.SemaphoreType.DMA((4, 6)),
            pltpu.SemaphoreType.DMA((4, 6)),
        ],
        compiler_params=pltpu.CompilerParams(
            collective_id=0, has_side_effects=True, vmem_limit_bytes=56 * 1024 * 1024
        ),
    )(
        composition,
        cotangent,
        weight_one,
        bias_one.reshape(1, h1),
        weight_two,
        bias_two.reshape(1, h2),
        weight_three,
        bias_three.reshape(1, mm),
    )
    cells = nx * ny * nz
    for a in axes:
        cells = cells * lax.axis_size(a)
    pay = lax.psum(pay, axes) * (1.0 / (step_size * math.sqrt(cells)))
    at = h1 + nc
    return (
        result,
        pay[h1 : 2 * h1, h1 : h1 + nc],
        pay[h1 : 2 * h1, at],
        pay[0:h1, h1:],
        pay[h1 : 2 * h1, at + 1],
        pay[:, 0:h1],
        jnp.concatenate(
            [pay[h1 : 2 * h1, at + 2], pay[h1 : 2 * h1, at + 3], pay[2 * h1 : mm, h1]]
        ),
    )


def solution(mesh):
    in_specs = (P(None, "gx", "gy", "gz"), P(None, "gx", "gy", "gz"), P(), P(), P(), P(), P(), P())
    out_specs = (P(None, "gx", "gy", "gz"), P(), P(), P(), P(), P(), P())
    return jax.shard_map(shards, mesh=mesh, in_specs=in_specs, out_specs=out_specs, check_vma=False)
```

time: 188 us -> 175 us (0.931)
  waiting for transfers between devices: 29.6 us -> 123 us
  local copies, waits for them, and re-layouts: 51.3 us -> 6.59 us
  blocking collectives: 42.9 us -> 0 us
  Pallas kernels: 0 us -> 29.5 us
  other arithmetic: 26.2 us -> 1.53 us
  matrix products: 17.5 us -> 0 us
  starting transfers between devices: 16.8 us -> 0.04 us
  between operations: 1.87 us -> 14 us
    psum x0 -> x1, waiting for transfers between devices: none -> 123 us  [shards(): pay = lax.psum(pay, axes) * (1.0 / (step_size * math.sqrt(cells)))]
    psum x1 -> x0, blocking collectives: 42.9 us -> none  [shards(): lax.psum((grads_late[0], grads_late[1], grads_late[2], grads_late[3], gra...]
    ppermute x18 -> x0, waiting for transfers between devices: 29.6 us -> none  [the longest x9 24 us: extended_2(): before = lax.ppermute(last, axis, up)]
    pallas_call x0 -> x1, Pallas kernels: none -> 29.5 us  [shards(): pl.pallas_call(functools.partial(kernel, (nc, nx, ny, nz, h1, h2)), out_s...]
    dot_general x22 -> x0, matrix products: 17.5 us -> none  [the longest x4 5.89 us: forward_net(): jnp.dot(weight_three, hidden_two, preferred_element_type=jnp.float32)]
    unnamed x196 -> x7, local copies, waits for them, and re-layouts: 21.9 us -> 4.9 us
    ppermute x18 -> x0, starting transfers between devices: 16.8 us -> none  [the longest x9 9.38 us: extended_2(): after = lax.ppermute(leading, axis, down)]
    concatenate x13 -> x0, local copies, waits for them, and re-layouts: 11.9 us -> none  [the longest x8 9.13 us: joined(): jnp.concatenate([jnp.expand_dims(lower_slab, spatial), inner_mob, jnp.exp...]
  transfers between devices with their start and end apart: 18 -> 1, of which waited for: 10 -> 1; matrix products, arithmetic and copies ran while one was open for 8% -> 0% of each run, Pallas kernels for 0% -> 0%
where the time goes in v1:
time: 175 us; the launch traced here: 174 us
  waiting for transfers between devices  123 us (70%)
  Pallas kernels  29.5 us (17%)
  between operations  14 us (8%)
  local copies, waits for them, and re-layouts  6.59 us (4%)
    psum x1, waiting for transfers between devices, shards(): pay = lax.psum(pay, axes) * (1.0 / (step_size * math.sqrt(cells)))  123 us
    pallas_call x1, Pallas kernels, shards(): pl.pallas_call(functools.partial(kernel, (nc, nx, ny, nz, h1, h2)), out_s...  29.5 us
    unnamed x7, local copies, waits for them, and re-layouts  4.9 us
  transfers between devices with their start and end apart: 1, of which 1 were waited for; matrix products, arithmetic and copies ran while one was open for 0% of the time, Pallas kernels for 0%

profile of v1, /device:TPU:12, one launch (start us, length us, event | category | flops | bytes accessed | tf_op | source)
XLA Modules:
  0.0 174.4 jit_solution(3914410006826176779)
XLA Ops:
  7.2 0.0 all-reduce.2.cloned.1.call-start
  7.2 1.4 copy.19.w1
  8.6 1.5 copy.20.w3
  10.1 29.5 %shard_map.135 = (f32[12,2,8,128]{3,2,1,0:T(8,128)}, f32[144,128]{1,0:T(8,128)}) custom-call(f32[12,2,8,128]{3,2,1,0:T(8,128)} %comp.1, f32[12,2,8,128]{3,2,1,0:T(8,128)} %cot.1, bf16[64,12]{1,0:T(8,128)(2,1)} %copy.19.w1, f32[1,64]{1,0:T(1,128)} %bitcast.6, bf16[64,64]{1,0:T(8,128)(2,1)} %w2.1, f32[1,64]{1,0:T(1,128)} %bitcast.7, bf16[144,64]{1,0:T(8,128)(2,1)} %copy.20.w3, ...), custom_call_target="tpu_custom_call" | custom-call | tf_op jit(solution)/shard_map/pallas_call | solution.py:437
  39.6 0.0 all-reduce.2.cloned.1.call-update
  39.6 122.6 %all-reduce.2.cloned.1.call-done = f32[144,128]{1,0:T(8,128)} async-done(((f32[144,128]{1,0:T(8,128)}), f32[144,128]{1,0:T(8,128)}) %all-reduce.2.cloned.1.call-update) | async-done | bytes 73744 | tf_op jit(solution)/shard_map/psum | solution.py:499
  162.3 0.9 broadcast_multiply_fusion
  163.2 0.2 slice_reduce_fusion.4
  163.3 0.7 slice_reduce_fusion.1
  164.1 0.7 slice.34
  164.8 0.1 slice.32
  164.8 0.0 copy-start
  164.9 0.7 copy.21
  165.5 0.7 copy.22
  166.2 0.6 pad_maximum_fusion
  166.9 0.0 copy-done
  166.9 0.6 copy.25
Async XLA Ops:
  7.2 155.1 %all-reduce.2.cloned.1.call-start = ((), (), s32[]{:S(2)}) async-start(), calls=%async_computation | async-start | bytes 147456 | tf_op jit(solution)/shard_map/psum | solution.py:499
  164.8 2.0 %copy-start = (f32[12,2,8,128]{3,2,1,0:T(8,128)S(1)}, f32[12,2,8,128]{3,2,1,0:T(8,128)}, u32[]{:S(2)}) copy-start(f32[12,2,8,128]{3,2,1,0:T(8,128)} %get-tuple-element.36) | copy-start | bytes 294916
Sparse Core Ops, SparseCore 0:
  39.7 122.4 all-reduce.1
